TPU v7x, 32 devices: a whole 2x2x4 slice. The times are simulated.
32 devices in a mesh: groups: 2 (over y), sec: 16 (over z, x, core).
Axes of the slice: x: 2, y: 2, z: 4, core: 2. Of those that a mesh axis runs over, the one named last changes fastest.
Arguments:
- psi: bfloat16 [4096, 64, 128], P(('groups', 'sec')), parts along dimension 0, may hold values from -6 to 6
- block_rows: int32 [4096], P(('groups', 'sec')), parts along dimension 0, may hold values from 1 to 64, as said below
- owner: int32 [4096, 1], P(('groups', 'sec')), parts along dimension 0, may hold values from 0 to 15; in each aligned block of 128 rows (0 to 127, 128 to 255, ...) at most 16 rows name the same one
- left_sector: int32 [4096], P(('groups', 'sec')), parts along dimension 0, may hold values from 0 to 3
- right_sector: int32 [4096], P(('groups', 'sec')), parts along dimension 0, may hold values from 0 to 31
- left_env: bfloat16 [128, 3, 64, 64], P(('groups', 'sec')), parts along dimension 0, may hold values from -0.75 to 0.75
- right_env: bfloat16 [1024, 2, 128, 128], P(('groups', 'sec')), parts along dimension 0, may hold values from -0.5 to 0.5
Outputs:
- h_psi: bfloat16 [4096, 64, 128], P(('groups', 'sec')), parts along dimension 0
There are 2 independent parts, one for each index of `groups`. A program takes and returns all parts, laid end to end along the dimension named above; each array names one. Nothing has to cross between parts.
Inputs may be any that keep to these rules, and one draw needn't show every extreme that they name: `block_rows`: the first block of the part has a full left sector of 64 rows. Among the blocks of one device, at most 16 name the same owner, a bound that some block reaches.
All inputs are finite; a program needn't handle non-finite values.
Results may differ from a plain program's by a relative error of at most 0.0043.
Values may be sent and summed in bfloat16 or wider, within the bound.
A program may use at most 128 MiB of HBM per device.

v0:
```python
import jax
import jax.numpy as jnp
from jax import lax
from jax.sharding import PartitionSpec as P


def shards(psi, block_rows, owner, left_sector, right_sector, left_env, right_env):
    blocks, rows_left, cols_right = psi.shape
    peers = lax.axis_size("sec")
    cap = max(2, 2 * blocks // peers)
    valid = jnp.arange(rows_left, dtype=jnp.int32)[None, :] < block_rows[:, None]
    masked = jnp.where(valid[:, :, None], psi, jnp.zeros((), psi.dtype))
    lenv = left_env[left_sector]
    moved = jnp.einsum(
        "bkij,bjc->bkic", lenv[:, 1:], masked, preferred_element_type=jnp.float32
    ).astype(jnp.bfloat16)
    terms = moved.shape[1]
    target = owner[:, 0]
    order = jnp.arange(blocks, dtype=jnp.int32)
    same = target[:, None] == target[None, :]
    earlier = order[None, :] < order[:, None]
    slot = jnp.sum(jnp.where(same & earlier, 1, 0), axis=1).astype(jnp.int32)
    position = target * cap + slot
    slots_all = jnp.arange(peers * cap, dtype=jnp.int32)
    match = position[None, :] == slots_all[:, None]
    source = jnp.sum(jnp.where(match, order[None, :], 0), axis=1)
    filled = jnp.any(match, axis=1)
    outgoing = jnp.where(filled[:, None, None, None], moved[source], jnp.zeros((), moved.dtype))
    outgoing = outgoing.reshape(peers, cap, terms, rows_left, cols_right)
    sector_tag = jnp.where(filled, right_sector[source], 0).reshape(peers, cap)
    arrived = lax.all_to_all(outgoing, "sec", split_axis=0, concat_axis=0, tiled=True)
    tags = lax.all_to_all(sector_tag, "sec", split_axis=0, concat_axis=0, tiled=True)
    renv = right_env[tags]
    summed = jnp.einsum("nckij,nckjl->ncil", arrived, renv, preferred_element_type=jnp.float32)
    returned = lax.all_to_all(summed, "sec", split_axis=0, concat_axis=0, tiled=True)
    far = returned.reshape(peers * cap, rows_left, cols_right)[position]
    local = jnp.einsum("bij,bjc->bic", lenv[:, 0], masked, preferred_element_type=jnp.float32)
    result = jnp.where(valid[:, :, None], local + far, jnp.float32(0.0))
    return result.astype(jnp.bfloat16)


def solution(mesh):
    return jax.shard_map(
        shards,
        mesh=mesh,
        in_specs=(
            P(("groups", "sec"), None, None),
            P(("groups", "sec")),
            P(("groups", "sec"), None),
            P(("groups", "sec")),
            P(("groups", "sec")),
            P(("groups", "sec"), None, None, None),
            P(("groups", "sec"), None, None, None),
        ),
        out_specs=P(("groups", "sec"), None, None),
        check_vma=False,
    )
```

profile of v0, /device:TPU:15, one launch (start us, length us, event | category | flops | bytes accessed | tf_op | source)
XLA Modules:
  0.0 443.0 jit_solution(16263248437643938834)
XLA Ops:
  0.0 1.0 select_reduce_fusion.1
  1.0 0.7 multiply_add_fusion
  1.7 0.1 select_reduce_fusion
  1.8 0.1 fusion.3
  1.9 1.9 gather_fusion.2
  3.8 0.7 select_n.71
  4.5 6.6 %all-to-all-start.1 = ((s32[16,1,16]{2,1,0:T(1,128)}), s32[16,1,16]{2,1,0:T(1,128)S(1)}, u32[]{:S(2)}, u32[]{:S(2)}) async-start(s32[16,1,16]{2,1,0:T(1,128)} %select_n.71), calls=%async_computation.1 | async-start | bytes 16384 | tf_op jit(solution)/shard_map/all_to_all | solution.py:32
  11.1 0.1 broadcast_in_dim.80
  11.2 0.7 compare_select_fusion.3
  11.8 0.7 iota_compare_fusion.2
  12.6 4.9 %gather_fusion = bf16[128,3,64,64]{3,2,1,0:T(8,128)(2,1)} fusion(bf16[4,3,64,64]{3,2,1,0:T(8,128)(2,1)} %param.12, s32[1024]{0:T(1024)S(1)} %pad_clamp_fusion.3), kind=kCustom, calls=%fused_computation | custom fusion | bytes 6291968 | tf_op jit(solution)/shard_map/gather | solution.py:13
  17.5 4.9 %convolution_convert_fusion = bf16[128,2,64,128]{3,2,1,0:T(8,128)(2,1)} fusion(bf16[128,3,64,64]{3,2,1,0:T(8,128)(2,1)} %gather_fusion, bf16[128,64,128]{2,1,0:T(8,128)(2,1)} %param.7, pred[128,64]{1,0:T(8,128)(4,1)S(1)} %iota_compare_fusion.2), kind=kOutput, calls=%fused_computation.8 | convolution fusion | flops 271581184 | bytes 9445376 | tf_op jit(solution)/shard_map/bkij,bjc->bkic/dot_general | solution.py:14
  22.3 10.7 %gather_fusion.1 = bf16[256,2,64,128]{3,2,1,0:T(8,128)(2,1)} fusion(bf16[128,2,64,128]{3,2,1,0:T(8,128)(2,1)} %convolution_convert_fusion, s32[1024]{0:T(1024)S(1)} %pad_clamp_fusion.2), kind=kCustom, calls=%fused_computation.1 | custom fusion | bytes 16778240 | tf_op jit(solution)/shard_map/gather | solution.py:28
  33.0 7.2 %broadcast_select_fusion = bf16[16,16,2,64,128]{4,3,2,1,0:T(8,128)(2,1)} fusion(bf16[16,16,2,64,128]{4,3,2,1,0:T(8,128)(2,1)} %bitcast.33, pred[16,16]{1,0:T(8,128)(4,1)S(1)} %broadcast_in_dim.80), kind=kLoop, calls=%fused_computation.5 | loop fusion | flops 4194304 | bytes 16777472 | tf_op jit(solution)/shard_map/jit(_where)/select_n | solution.py:28
  40.2 0.0 all-to-all-done.1
  40.2 6.0 %all-to-all-start = ((bf16[16,16,2,64,128]{4,3,2,1,0:T(8,128)(2,1)}), bf16[16,16,2,64,128]{4,3,2,1,0:T(8,128)(2,1)}, u32[]{:S(2)}, u32[]{:S(2)}) async-start(bf16[16,16,2,64,128]{4,3,2,1,0:T(8,128)(2,1)} %broadcast_select_fusion), calls=%async_computation | async-start | bytes 16777216 | tf_op jit(solution)/shard_map/all_to_all | solution.py:31
  46.3 0.1 reshape.131
  46.4 9.2 %gather_fusion.3 = bf16[256,2,128,128]{3,2,1,0:T(8,128)(2,1)} fusion(bf16[32,2,128,128]{3,2,1,0:T(8,128)(2,1)S(1)} %copy-done, s32[1024]{0:T(1024)S(1)} %pad_clamp_fusion.1), kind=kCustom, calls=%fused_computation.3 | custom fusion | bytes 33555456 | tf_op jit(solution)/shard_map/gather | solution.py:33
  55.6 173.0 %all-to-all-done = bf16[16,16,2,64,128]{4,3,2,1,0:T(8,128)(2,1)} async-done(((bf16[16,16,2,64,128]{4,3,2,1,0:T(8,128)(2,1)}), bf16[16,16,2,64,128]{4,3,2,1,0:T(8,128)(2,1)}, u32[]{:S(2)}, u32[]{:S(2)}) %all-to-all-start) | async-done | bytes 8388640 | tf_op jit(solution)/shard_map/all_to_all | solution.py:31
  228.6 14.4 %convolution_bitcast_fusion = f32[16,16,64,128]{3,2,1,0:T(8,128)} fusion(bf16[16,16,2,64,128]{4,3,2,1,0:T(8,128)(2,1)} %all-to-all-done, bf16[16,16,2,128,128]{4,3,2,1,0:T(8,128)(2,1)} %bitcast.32), kind=kOutput, calls=%fused_computation.7 | convolution fusion | flops 1073741824 | bytes 33554432 | tf_op jit(solution)/shard_map/nckij,nckjl->ncil/dot_general | solution.py:34
  243.0 5.0 %all-to-all-start.2 = ((f32[16,16,64,128]{3,2,1,0:T(8,128)}), f32[16,16,64,128]{3,2,1,0:T(8,128)}, u32[]{:S(2)}, u32[]{:S(2)}) async-start(f32[16,16,64,128]{3,2,1,0:T(8,128)} %convolution_bitcast_fusion), calls=%async_computation.2 | async-start | bytes 16777216 | tf_op jit(solution)/shard_map/all_to_all | solution.py:35
  248.1 182.3 %all-to-all-done.2 = f32[16,16,64,128]{3,2,1,0:T(8,128)} async-done(((f32[16,16,64,128]{3,2,1,0:T(8,128)}), f32[16,16,64,128]{3,2,1,0:T(8,128)}, u32[]{:S(2)}, u32[]{:S(2)}) %all-to-all-start.2) | async-done | bytes 8388640 | tf_op jit(solution)/shard_map/all_to_all | solution.py:35
  430.4 6.3 %gather_fusion.4 = f32[128,64,128]{2,1,0:T(8,128)} fusion(f32[256,64,128]{2,1,0:T(8,128)} %bitcast.11, s32[1024]{0:T(1024)S(1)} %pad_clamp_fusion), kind=kCustom, calls=%fused_computation.4 | custom fusion | bytes 8389120 | tf_op jit(solution)/shard_map/gather | solution.py:36
  436.7 6.2 %select_convert_fusion = bf16[128,64,128]{2,1,0:T(8,128)(2,1)} fusion(f32[128,64,128]{2,1,0:T(8,128)} %gather_fusion.4, bf16[128,3,64,64]{3,2,1,0:T(8,128)(2,1)} %gather_fusion, pred[128,64]{1,0:T(8,128)(4,1)S(1)} %iota_compare_fusion.2, bf16[128,64,128]{2,1,0:T(8,128)(2,1)} %param.7), kind=kOutput, calls=%fused_computation.6 | convolution fusion | flops 138412032 | bytes 10518528 | tf_op jit(solution)/shard_map/bij,bjc->bic/dot_general | solution.py:37
  (14 shorter events, 0.1 us)
Async XLA Ops:
  0.0 46.4 %copy-start = (bf16[32,2,128,128]{3,2,1,0:T(8,128)(2,1)S(1)}, bf16[32,2,128,128]{3,2,1,0:T(8,128)(2,1)}, u32[]{:S(2)}) copy-start(bf16[32,2,128,128]{3,2,1,0:T(8,128)(2,1)} %param.13) | copy-start | bytes 6291460
  4.5 35.7 %all-to-all-start.1 = ((s32[16,1,16]{2,1,0:T(1,128)}), s32[16,1,16]{2,1,0:T(1,128)S(1)}, u32[]{:S(2)}, u32[]{:S(2)}) async-start(s32[16,1,16]{2,1,0:T(1,128)} %select_n.71), calls=%async_computation.1 | async-start | bytes 16384 | tf_op jit(solution)/shard_map/all_to_all | solution.py:32
  40.2 188.4 %all-to-all-start = ((bf16[16,16,2,64,128]{4,3,2,1,0:T(8,128)(2,1)}), bf16[16,16,2,64,128]{4,3,2,1,0:T(8,128)(2,1)}, u32[]{:S(2)}, u32[]{:S(2)}) async-start(bf16[16,16,2,64,128]{4,3,2,1,0:T(8,128)(2,1)} %broadcast_select_fusion), calls=%async_computation | async-start | bytes 16777216 | tf_op jit(solution)/shard_map/all_to_all | solution.py:31
  243.0 5.0 %copy-start.2 = (s32[128,1]{0,1:T(1,128)S(1)}, s32[128,1]{0,1:T(1,128)}, u32[]{:S(2)}) copy-start(s32[128,1]{0,1:T(1,128)} %param.9) | copy-start | bytes 1540
  243.0 187.4 %all-to-all-start.2 = ((f32[16,16,64,128]{3,2,1,0:T(8,128)}), f32[16,16,64,128]{3,2,1,0:T(8,128)}, u32[]{:S(2)}, u32[]{:S(2)}) async-start(f32[16,16,64,128]{3,2,1,0:T(8,128)} %convolution_bitcast_fusion), calls=%async_computation.2 | async-start | bytes 16777216 | tf_op jit(solution)/shard_map/all_to_all | solution.py:35
  430.4 12.6 %copy-start.1 = (bf16[32,2,128,128]{3,2,1,0:T(8,128)(2,1)S(1)}, bf16[32,2,128,128]{3,2,1,0:T(8,128)(2,1)}, u32[]{:S(2)}) copy-start(bf16[32,2,128,128]{3,2,1,0:T(8,128)(2,1)} %param.13) | copy-start | bytes 6291460
where the time goes:
time: 444 us; the launch traced here: 443 us
  waiting for transfers between devices  355 us (80%)
  local copies, waits for them, and re-layouts  33.8 us (8%)
  matrix products  25.5 us (6%)
  starting transfers between devices  17.6 us (4%)
  other arithmetic  10.6 us (2%)
    all_to_all x1, waiting for transfers between devices, shards(): lax.all_to_all(summed, 'sec', split_axis=0, concat_axis=0, tiled=True)  182 us
    all_to_all x1, waiting for transfers between devices, shards(): lax.all_to_all(outgoing, 'sec', split_axis=0, concat_axis=0, tiled=True)  173 us
    dot_general x1, matrix products, shards(): jnp.einsum('nckij,nckjl->ncil', arrived, renv, preferred_element_type=jnp...  14.4 us
    gather x1, local copies, waits for them, and re-layouts, shards(): moved[source]  10.7 us
    gather x1, local copies, waits for them, and re-layouts, shards(): renv = right_env[tags]  9.21 us
  transfers between devices with their start and end apart: 3, of which 2 were waited for; matrix products, arithmetic and copies ran while one was open for 9% of the time, Pallas kernels for 0%

commit v1 on v0

v1 whole, which is shorter than its diff:
```python
import functools

import jax
import jax.numpy as jnp
from jax import lax
from jax.experimental import pallas as pl
from jax.experimental.pallas import tpu as pltpu
from jax.sharding import PartitionSpec as P


def apply_kernel(step, cap, lsec, terms, lsel, rsel, rows, psi_ref, left_ref, right_ref, out_ref):
    bl, br = psi_ref.shape[1:]
    line = lax.broadcasted_iota(jnp.int32, (bl, br), 0)
    base = pl.program_id(0) * step
    for g in range(step):
        slot = base + g
        peer = slot // cap
        keep = line < rows[slot]
        block = jnp.where(keep, psi_ref[g], jnp.zeros((), psi_ref.dtype))
        left = left_ref[peer * lsec + lsel[slot]]
        made = jnp.dot(left, block, preferred_element_type=jnp.float32)
        moved = jnp.concatenate(
            [made[(k + 1) * bl:(k + 2) * bl].astype(jnp.bfloat16) for k in range(terms)], axis=1
        )
        far = jnp.dot(moved, right_ref[rsel[slot]], preferred_element_type=jnp.float32)
        out_ref[g] = jnp.where(keep, made[:bl] + far, jnp.float32(0.0)).astype(out_ref.dtype)


def apply_blocks(blocks, tags, left, right, peers, cap, lsec):
    slots, bl, br = blocks.shape
    rsec, terms = right.shape[:2]
    rows = tags % (bl + 1)
    lsel = (tags // (bl + 1)) % lsec
    rsel = tags // ((bl + 1) * lsec)
    step = 16
    left = left.reshape(peers * lsec, (terms + 1) * bl, bl)
    right = right.reshape(rsec, terms * br, br)
    return pl.pallas_call(
        functools.partial(apply_kernel, step, cap, lsec, terms),
        grid_spec=pltpu.PrefetchScalarGridSpec(
            num_scalar_prefetch=3,
            grid=(slots // step,),
            in_specs=[
                pl.BlockSpec((step, bl, br), lambda i, *_: (i, 0, 0)),
                pl.BlockSpec(left.shape, lambda i, *_: (0, 0, 0)),
                pl.BlockSpec(right.shape, lambda i, *_: (0, 0, 0)),
            ],
            out_specs=pl.BlockSpec((step, bl, br), lambda i, *_: (i, 0, 0)),
        ),
        out_shape=jax.ShapeDtypeStruct(blocks.shape, jnp.bfloat16),
        compiler_params=pltpu.CompilerParams(vmem_limit_bytes=40 * 1024 * 1024),
        cost_estimate=pl.CostEstimate(
            flops=2 * slots * bl * br * ((terms + 1) * bl + terms * br),
            bytes_accessed=4 * slots * bl * br + 2 * left.size + 2 * right.size,
            transcendentals=0,
        ),
    )(lsel, rsel, rows, blocks, left, right)


def shards(psi, block_rows, owner, left_sector, right_sector, left_env, right_env):
    blocks, bl, br = psi.shape
    n = lax.axis_size("sec")
    half = n // 2
    cap = max(2, 2 * blocks // n)
    lsec = left_env.shape[0]
    groups = [list(range(half)), list(range(half, n))]
    mirrored = lax.ppermute(right_env, "sec", [(i, (i + half) % n) for i in range(n)])

    exchange = functools.partial(
        lax.all_to_all, axis_name="sec", split_axis=0, concat_axis=0, axis_index_groups=groups, tiled=True
    )
    mine = lax.axis_index("sec") // half
    target = owner[:, 0]
    order = jnp.arange(blocks, dtype=jnp.int32)
    same = target[:, None] == target[None, :]
    earlier = order[None, :] < order[:, None]
    slot = jnp.sum(jnp.where(same & earlier, 1, 0), axis=1).astype(jnp.int32)
    kind = jnp.where(target // half == mine, 0, 1)
    spot = (target % half) * cap + slot
    position = kind * (half * cap) + spot
    slots_all = jnp.arange(n * cap, dtype=jnp.int32)
    match = position[None, :] == slots_all[:, None]
    tag = (right_sector * lsec + left_sector) * (bl + 1) + block_rows
    source = jnp.sum(jnp.where(match, order[None, :], 0), axis=1)
    tags = jnp.sum(jnp.where(match, tag[None, :], 0), axis=1)

    sent = [psi[source[k * half * cap:(k + 1) * half * cap]] for k in range(2)]
    tags = exchange(tags.reshape(2, half, cap).transpose(1, 0, 2)).transpose(1, 0, 2).reshape(2, half * cap)
    left = lax.all_gather(left_env, "sec", axis_index_groups=groups, tiled=True)
    returned = []
    for k, right in enumerate((right_env, mirrored)):
        arrived = exchange(sent[k].reshape(half, cap, bl, br)).reshape(half * cap, bl, br)
        done = apply_blocks(arrived, tags[k], left, right, half, cap, lsec)
        returned.append(exchange(done.reshape(half, cap, bl, br)).reshape(half * cap, bl, br))
    near = returned[0][jnp.where(kind == 0, spot, 0)]
    far = returned[1][jnp.where(kind == 0, 0, spot)]
    return jnp.where((kind == 0)[:, None, None], near, far)


def solution(mesh):
    return jax.shard_map(
        shards,
        mesh=mesh,
        in_specs=(
            P(("groups", "sec"), None, None),
            P(("groups", "sec")),
            P(("groups", "sec"), None),
            P(("groups", "sec")),
            P(("groups", "sec")),
            P(("groups", "sec"), None, None, None),
            P(("groups", "sec"), None, None, None),
        ),
        out_specs=P(("groups", "sec"), None, None),
        check_vma=False,
    )
```

time: 444 us -> 244 us (0.55)
  the two profiles are of different devices: /device:TPU:15 before, /device:TPU:0 now
where the time goes in v1:
time: 244 us; the launch traced here: 243 us
  blocking collectives  99.8 us (41%)
  waiting for transfers between devices  47.9 us (20%)
  Pallas kernels  42.8 us (18%)
  starting transfers between devices  25.6 us (10%)
  local copies, waits for them, and re-layouts  20.3 us (8%)
  other arithmetic  6.7 us (3%)
    all_gather x1, blocking collectives, shards(): left = lax.all_gather(left_env, 'sec', axis_index_groups=groups, tiled=True)  99.8 us
    pallas_call x2, Pallas kernels, apply_blocks(): pl.pallas_call(functools.partial(apply_kernel, step, cap, lsec, terms), g...  42.8 us
    all_to_all x2, waiting for transfers between devices, shards(): exchange(sent[k].reshape(half, cap, bl, br)).reshape(half * cap, bl, br)  23.5 us
    all_to_all x2, waiting for transfers between devices, shards(): exchange(done.reshape(half, cap, bl, br)).reshape(half * cap, bl, br)  21.9 us
    all_to_all x2, starting transfers between devices, shards(): exchange(done.reshape(half, cap, bl, br)).reshape(half * cap, bl, br)  8.85 us
    all_to_all x2, starting transfers between devices, shards(): exchange(sent[k].reshape(half, cap, bl, br)).reshape(half * cap, bl, br)  8.84 us
    unnamed x16, local copies, waits for them, and re-layouts  7.04 us
    all_to_all x1, starting transfers between devices, shards(): exchange(tags.reshape(2, half, cap).transpose(1, 0, 2)).transpose(1, 0, 2)  5.23 us
  transfers between devices with their start and end apart: 6, of which 3 were waited for; matrix products, arithmetic and copies ran while one was open for 4% of the time, Pallas kernels for 18%

profile of v1, /device:TPU:0, one launch (start us, length us, event | category | flops | bytes accessed | tf_op | source)
XLA Modules:
  0.0 243.4 jit_solution(910294203647448457)
XLA Ops:
  0.0 0.8 broadcast_compare_fusion
  0.8 0.9 select_reduce_fusion.2
  3.3 5.2 %all-to-all-start = ((s32[8,2,16]{2,1,0:T(2,128)}), s32[8,2,16]{2,1,0:T(2,128)S(1)}, u32[]{:S(2)}, u32[]{:S(2)}) async-start(s32[8,2,16]{2,1,0:T(2,128)} %copy.9), calls=%async_computation | async-start | bytes 16384 | tf_op jit(solution)/shard_map/all_to_all | solution.py:88
  8.6 2.2 gather_fusion.2
  10.7 2.5 %all-to-all-done = s32[8,2,16]{2,1,0:T(2,128)S(1)} async-done(((s32[8,2,16]{2,1,0:T(2,128)}), s32[8,2,16]{2,1,0:T(2,128)S(1)}, u32[]{:S(2)}, u32[]{:S(2)}) %all-to-all-start) | async-done | bytes 1056 | tf_op jit(solution)/shard_map/all_to_all | solution.py:88
  13.2 4.4 %all-to-all-start.3 = ((bf16[8,16,64,128]{3,2,1,0:T(8,128)(2,1)}), bf16[8,16,64,128]{3,2,1,0:T(8,128)(2,1)}, u32[]{:S(2)}, u32[]{:S(2)}) async-start(bf16[8,16,64,128]{3,2,1,0:T(8,128)(2,1)} %bitcast.34), calls=%async_computation.3 | async-start | bytes 4194304 | tf_op jit(solution)/shard_map/all_to_all | solution.py:92
  17.6 2.1 gather_fusion
  19.7 23.5 %all-to-all-done.3 = bf16[8,16,64,128]{3,2,1,0:T(8,128)(2,1)} async-done(((bf16[8,16,64,128]{3,2,1,0:T(8,128)(2,1)}), bf16[8,16,64,128]{3,2,1,0:T(8,128)(2,1)}, u32[]{:S(2)}, u32[]{:S(2)}) %all-to-all-start.3) | async-done | bytes 2097184 | tf_op jit(solution)/shard_map/all_to_all | solution.py:92
  43.3 4.5 %all-to-all-start.1 = ((bf16[8,16,64,128]{3,2,1,0:T(8,128)(2,1)}), bf16[8,16,64,128]{3,2,1,0:T(8,128)(2,1)}, u32[]{:S(2)}, u32[]{:S(2)}) async-start(bf16[8,16,64,128]{3,2,1,0:T(8,128)(2,1)} %bitcast.33), calls=%async_computation.1 | async-start | bytes 4194304 | tf_op jit(solution)/shard_map/all_to_all | solution.py:92
  47.8 2.7 %collective-permute-start = (bf16[32,2,128,128]{3,2,1,0:T(8,128)(2,1)}, bf16[32,2,128,128]{3,2,1,0:T(8,128)(2,1)}, u32[]{:S(2)}, u32[]{:S(2)}) collective-permute-start(bf16[32,2,128,128]{3,2,1,0:T(8,128)(2,1)} %param.13), channel_id=1, source_target_pairs={{0,8},{1,9},{2,10},{3,11},{4,12},{5,13},{6,14},{7,15},{8,0},{9,1},... | collective-permute-start | bytes 6291464 | tf_op jit(solution)/shard_map/ppermute | solution.py:67
  50.4 99.8 %all_gather.3 = bf16[32,3,64,64]{3,2,1,0:T(8,128)(2,1)} all-gather(bf16[4,3,64,64]{3,2,1,0:T(8,128)(2,1)S(1)} %copy-done.6), channel_id=1, replica_groups={{0,1,2,3,4,5,6,7},{8,9,10,11,12,13,14,15},{16,17,18,19,20,21,22,23},{24..., dimensions={0}, use_global_device_ids=true | all-gather | bytes 884736 | tf_op jit(solution)/shard_map/all_gather | solution.py:89
  150.9 1.4 copy-done.1
  152.3 21.8 %shard_map.74 = bf16[128,64,128]{2,1,0:T(8,128)(2,1)S(1)} custom-call(s32[128]{0:T(128)S(1)} %get-tuple-element.25.lsel, s32[128]{0:T(128)S(1)} %get-tuple-element.26.rsel, s32[128]{0:T(128)S(1)} %get-tuple-element.24.rows, bf16[128,64,128]{2,1,0:T(8,128)(2,1)} %bitcast.12.psi_ref, bf16[32,192,64]{2,1,0:T(8,128)(2,1)S(1)} %bitcast.28, ...), custom_call_target="tpu_custom_call" | custom-call | flops 939524096 | bytes 7077888 | tf_op jit(solution)/shard_map/pallas_call | solution.py:38
  174.1 1.3 copy-done.3
  175.4 4.4 %all-to-all-start.4 = ((bf16[8,16,64,128]{3,2,1,0:T(8,128)(2,1)}), bf16[8,16,64,128]{3,2,1,0:T(8,128)(2,1)}, u32[]{:S(2)}, u32[]{:S(2)}) async-start(bf16[8,16,64,128]{3,2,1,0:T(8,128)(2,1)} %bitcast.30), calls=%async_computation.4 | async-start | bytes 4194304 | tf_op jit(solution)/shard_map/all_to_all | solution.py:94
  180.3 1.4 copy-done.2
  181.7 1.6 copy-done.5
  183.3 21.0 %shard_map.73 = bf16[128,64,128]{2,1,0:T(8,128)(2,1)S(1)} custom-call(s32[128]{0:T(128)S(1)} %get-tuple-element.28.lsel, s32[128]{0:T(128)S(1)} %get-tuple-element.29.rsel, s32[128]{0:T(128)S(1)} %get-tuple-element.27.rows, bf16[128,64,128]{2,1,0:T(8,128)(2,1)} %bitcast.4.psi_ref, bf16[32,192,64]{2,1,0:T(8,128)(2,1)S(1)} %bitcast.29, ...), custom_call_target="tpu_custom_call" | custom-call | flops 939524096 | bytes 7077888 | tf_op jit(solution)/shard_map/pallas_call | solution.py:38
  204.3 1.3 copy-done.4
  205.6 4.5 %all-to-all-start.2 = ((bf16[8,16,64,128]{3,2,1,0:T(8,128)(2,1)}), bf16[8,16,64,128]{3,2,1,0:T(8,128)(2,1)}, u32[]{:S(2)}, u32[]{:S(2)}) async-start(bf16[8,16,64,128]{3,2,1,0:T(8,128)(2,1)} %bitcast.31), calls=%async_computation.2 | async-start | bytes 4194304 | tf_op jit(solution)/shard_map/all_to_all | solution.py:94
  210.2 3.7 %gather_fusion.3 = bf16[128,64,128]{2,1,0:T(8,128)(2,1)} fusion(bf16[128,64,128]{2,1,0:T(8,128)(2,1)} %bitcast.15, s32[1024]{0:T(1024)S(1)} %pad_clamp_fusion), kind=kCustom, calls=%fused_computation.3 | custom fusion | bytes 4194816 | tf_op jit(solution)/shard_map/gather | solution.py:96
  213.9 21.9 %all-to-all-done.2 = bf16[8,16,64,128]{3,2,1,0:T(8,128)(2,1)} async-done(((bf16[8,16,64,128]{3,2,1,0:T(8,128)(2,1)}), bf16[8,16,64,128]{3,2,1,0:T(8,128)(2,1)}, u32[]{:S(2)}, u32[]{:S(2)}) %all-to-all-start.2) | async-done | bytes 2097184 | tf_op jit(solution)/shard_map/all_to_all | solution.py:94
  235.8 3.7 %gather_fusion.1 = bf16[128,64,128]{2,1,0:T(8,128)(2,1)} fusion(bf16[128,64,128]{2,1,0:T(8,128)(2,1)} %bitcast.8, s32[1024]{0:T(1024)S(1)} %pad_clamp_fusion.2), kind=kCustom, calls=%fused_computation.1 | custom fusion | bytes 4194816 | tf_op jit(solution)/shard_map/gather | solution.py:95
  239.5 3.8 %broadcast_select_fusion = bf16[128,64,128]{2,1,0:T(8,128)(2,1)} fusion(bf16[128,64,128]{2,1,0:T(8,128)(2,1)} %gather_fusion.1, bf16[128,64,128]{2,1,0:T(8,128)(2,1)} %gather_fusion.3, pred[128]{0:T(512)(128)(4,1)S(1)} %get-tuple-element.17), kind=kLoop, calls=%fused_computation.4 | loop fusion | flops 1048576 | bytes 6291584 | tf_op jit(solution)/shard_map/jit(_where)/select_n | solution.py:97
  (39 shorter events, 2.7 us)
Async XLA Ops:
  0.0 8.5 %copy-start = (bf16[128,64,128]{2,1,0:T(8,128)(2,1)S(1)}, bf16[128,64,128]{2,1,0:T(8,128)(2,1)}, u32[]{:S(2)}) copy-start(bf16[128,64,128]{2,1,0:T(8,128)(2,1)} %param.7) | copy-start | bytes 6291460
  3.3 9.9 %all-to-all-start = ((s32[8,2,16]{2,1,0:T(2,128)}), s32[8,2,16]{2,1,0:T(2,128)S(1)}, u32[]{:S(2)}, u32[]{:S(2)}) async-start(s32[8,2,16]{2,1,0:T(2,128)} %copy.9), calls=%async_computation | async-start | bytes 16384 | tf_op jit(solution)/shard_map/all_to_all | solution.py:88
  13.2 30.1 %all-to-all-start.3 = ((bf16[8,16,64,128]{3,2,1,0:T(8,128)(2,1)}), bf16[8,16,64,128]{3,2,1,0:T(8,128)(2,1)}, u32[]{:S(2)}, u32[]{:S(2)}) async-start(bf16[8,16,64,128]{3,2,1,0:T(8,128)(2,1)} %bitcast.34), calls=%async_computation.3 | async-start | bytes 4194304 | tf_op jit(solution)/shard_map/all_to_all | solution.py:92
  43.3 7.1 %copy-start.6 = (bf16[4,3,64,64]{3,2,1,0:T(8,128)(2,1)S(1)}, bf16[4,3,64,64]{3,2,1,0:T(8,128)(2,1)}, u32[]{:S(2)}) copy-start(bf16[4,3,64,64]{3,2,1,0:T(8,128)(2,1)} %param.12) | copy-start | bytes 294916
  43.3 132.2 %all-to-all-start.1 = ((bf16[8,16,64,128]{3,2,1,0:T(8,128)(2,1)}), bf16[8,16,64,128]{3,2,1,0:T(8,128)(2,1)}, u32[]{:S(2)}, u32[]{:S(2)}) async-start(bf16[8,16,64,128]{3,2,1,0:T(8,128)(2,1)} %bitcast.33), calls=%async_computation.1 | async-start | bytes 4194304 | tf_op jit(solution)/shard_map/all_to_all | solution.py:92
  47.8 103.1 %collective-permute-start = (bf16[32,2,128,128]{3,2,1,0:T(8,128)(2,1)}, bf16[32,2,128,128]{3,2,1,0:T(8,128)(2,1)}, u32[]{:S(2)}, u32[]{:S(2)}) collective-permute-start(bf16[32,2,128,128]{3,2,1,0:T(8,128)(2,1)} %param.13), channel_id=1, source_target_pairs={{0,8},{1,9},{2,10},{3,11},{4,12},{5,13},{6,14},{7,15},{8,0},{9,1},... | collective-permute-start | bytes 6291464 | tf_op jit(solution)/shard_map/ppermute | solution.py:67
  150.9 1.4 copy-start.1
  174.1 1.3 copy-start.3
  175.4 30.2 %all-to-all-start.4 = ((bf16[8,16,64,128]{3,2,1,0:T(8,128)(2,1)}), bf16[8,16,64,128]{3,2,1,0:T(8,128)(2,1)}, u32[]{:S(2)}, u32[]{:S(2)}) async-start(bf16[8,16,64,128]{3,2,1,0:T(8,128)(2,1)} %bitcast.30), calls=%async_computation.4 | async-start | bytes 4194304 | tf_op jit(solution)/shard_map/all_to_all | solution.py:94
  180.3 1.4 copy-start.2
  181.7 1.6 copy-start.5
  204.3 1.3 copy-start.4
  205.6 4.5 %copy-start.7 = (s32[128,1]{0,1:T(1,128)S(1)}, s32[128,1]{0,1:T(1,128)}, u32[]{:S(2)}) copy-start(s32[128,1]{0,1:T(1,128)} %param.9) | copy-start | bytes 1540
  205.6 30.2 %all-to-all-start.2 = ((bf16[8,16,64,128]{3,2,1,0:T(8,128)(2,1)}), bf16[8,16,64,128]{3,2,1,0:T(8,128)(2,1)}, u32[]{:S(2)}, u32[]{:S(2)}) async-start(bf16[8,16,64,128]{3,2,1,0:T(8,128)(2,1)} %bitcast.31), calls=%async_computation.2 | async-start | bytes 4194304 | tf_op jit(solution)/shard_map/all_to_all | solution.py:94

commit v2 on v0

v2 whole, which is shorter than its diff:
```python
import functools

import jax
import jax.numpy as jnp
from jax import lax
from jax.experimental import pallas as pl
from jax.experimental.pallas import tpu as pltpu
from jax.sharding import PartitionSpec as P

F32 = jnp.float32


def route_kernel(
    n, lsec,
    source, position, tags_in, psi, left_in, right_in,
    out,
    sent, got, back, total, right, mirror0, mirror1, left, tags_v, tags,
    psi_send, psi_recv, ret_send, ret_recv, tag_send, tag_recv, left_send, left_recv,
    mir_send, mir_recv, own_sem, tag_sem,
):
    half = n // 2
    cap, bl, br = sent.shape[2:]
    me = lax.axis_index("sec")
    first = (me // half) * half
    mine = me - first
    partner = lax.rem(me + half, n)

    barrier = pltpu.get_barrier_semaphore()

    def greet(j, c):
        pl.semaphore_signal(barrier, inc=1, device_id={"sec": first + lax.rem(mine + j, half)})
        return c

    lax.fori_loop(1, half, greet, 0)
    pl.semaphore_signal(barrier, inc=1, device_id={"sec": partner})
    pl.semaphore_wait(barrier, half)

    mirrors = (mirror0, mirror1)

    def mirror_copy(k):
        return pltpu.make_async_remote_copy(
            src_ref=right_in.at[:, k], dst_ref=mirrors[k], send_sem=mir_send.at[k],
            recv_sem=mir_recv.at[k], device_id={"sec": partner},
        )

    def tag_copy(to, slot):
        return pltpu.make_async_remote_copy(
            src_ref=tags_in.at[to], dst_ref=tags_v.at[slot], send_sem=tag_send.at[to],
            recv_sem=tag_recv.at[slot], device_id={"sec": first + to},
        )

    def left_copy(to, slot):
        return pltpu.make_async_remote_copy(
            src_ref=left_in, dst_ref=left.at[slot], send_sem=left_send.at[to],
            recv_sem=left_recv.at[slot], device_id={"sec": first + to},
        )

    def psi_copy(kind, to, slot):
        return pltpu.make_async_remote_copy(
            src_ref=sent.at[kind, to], dst_ref=got.at[kind, slot], send_sem=psi_send.at[kind, to],
            recv_sem=psi_recv.at[kind, slot], device_id={"sec": first + to},
        )

    def ret_copy(kind, to, slot):
        return pltpu.make_async_remote_copy(
            src_ref=got.at[kind, to], dst_ref=back.at[kind, slot], send_sem=ret_send.at[kind, to],
            recv_sem=ret_recv.at[kind, slot], device_id={"sec": first + to},
        )

    mirror_copy(0).start()
    mirror_copy(1).start()
    own = [
        pltpu.make_async_copy(right_in, right, own_sem.at[0]),
        pltpu.make_async_copy(left_in, left.at[mine], own_sem.at[1]),
        pltpu.make_async_copy(tags_in.at[mine], tags_v.at[mine], own_sem.at[2]),
    ]
    for copy in own:
        copy.start()

    def send_small(j, c):
        to = lax.rem(mine + j, half)
        tag_copy(to, mine).start()
        left_copy(to, mine).start()
        return c

    lax.fori_loop(1, half, send_small, 0)

    def pack(kind, dest, into):
        def one(s, c):
            into[kind, dest, s] = psi[source[(kind * half + dest) * cap + s]]
            return c
        lax.fori_loop(0, cap, one, 0, unroll=min(cap, 4))

    for kind in range(2):
        def send_psi(j, c):
            to = lax.rem(mine + j, half)
            pack(kind, to, sent)
            psi_copy(kind, to, mine).start()
            return c
        lax.fori_loop(1, half, send_psi, 0)
        pack(kind, mine, got)

    for copy in own:
        copy.wait()

    def take_small(j, c):
        src = lax.rem(mine + half - j, half)
        tag_copy(src, src).wait_recv()
        left_copy(src, src).wait_recv()
        return c

    lax.fori_loop(1, half, take_small, 0)
    copy = pltpu.make_async_copy(tags_v, tags, tag_sem)
    copy.start()
    copy.wait()

    group = min(cap, 8)
    line = lax.broadcasted_iota(jnp.int32, (bl, br), 0)

    def fields(kind, src, s):
        tag = tags[src, 0, kind * cap + s]
        return tag % (bl + 1), (tag // (bl + 1)) % lsec, tag // ((bl + 1) * lsec)

    def contract_left(kind, src, s):
        rows, lsel, _ = fields(kind, src, s)
        block = jnp.where(line < rows, got[kind, src, s], jnp.zeros((), jnp.bfloat16))
        packed = left[src, lsel]
        made = jnp.concatenate([
            jnp.dot(packed[:, :bl], block, preferred_element_type=F32),
            jnp.dot(packed[:, bl:], block, preferred_element_type=F32),
        ], axis=0)
        return made[:bl], made[bl:2 * bl].astype(jnp.bfloat16), made[2 * bl:].astype(jnp.bfloat16)

    def over_groups(work):
        def one(g, c):
            work([g * group + i for i in range(group)])
            return c
        lax.fori_loop(0, cap // group, one, 0)

    def whole(kind, src, into):
        def work(slots):
            parts = [contract_left(kind, src, s) for s in slots]
            for s, (local, m0, m1) in zip(slots, parts):
                rows, _, rsel = fields(kind, src, s)
                far = jnp.dot(m0, right[rsel, 0], preferred_element_type=F32)
                far = far + jnp.dot(m1, right[rsel, 1], preferred_element_type=F32)
                into[kind, src, s] = jnp.where(line < rows, local + far, 0.0).astype(jnp.bfloat16)
        over_groups(work)

    def first_term(src):
        def work(slots):
            parts = [contract_left(1, src, s) for s in slots]
            for s, (local, m0, m1) in zip(slots, parts):
                _, _, rsel = fields(1, src, s)
                total[src, s] = local + jnp.dot(m0, mirror0[rsel], preferred_element_type=F32)
                got[1, src, s] = m1
        over_groups(work)

    def second_term(src, into):
        def work(slots):
            for s in slots:
                rows, _, rsel = fields(1, src, s)
                far = total[src, s] + jnp.dot(got[1, src, s], mirror1[rsel], preferred_element_type=F32)
                into[1, src, s] = jnp.where(line < rows, far, 0.0).astype(jnp.bfloat16)
        over_groups(work)

    def serve_near(j, c):
        src = lax.rem(mine + half - j, half)
        psi_copy(0, src, src).wait_recv()
        whole(0, src, got)
        ret_copy(0, src, mine).start()
        return c

    lax.fori_loop(1, half, serve_near, 0)
    whole(0, mine, back)

    mirror_copy(0).wait_recv()

    def begin_far(j, c):
        src = lax.rem(mine + half - j, half)
        psi_copy(1, src, src).wait_recv()
        first_term(src)
        return c

    lax.fori_loop(1, half, begin_far, 0)
    first_term(mine)

    mirror_copy(1).wait_recv()

    def end_far(j, c):
        src = lax.rem(mine + half - j, half)
        second_term(src, got)
        ret_copy(1, src, mine).start()
        return c

    lax.fori_loop(1, half, end_far, 0)
    second_term(mine, back)

    def take_back(j, c):
        src = lax.rem(mine + half - j, half)
        ret_copy(0, src, src).wait_recv()
        ret_copy(1, src, src).wait_recv()
        return c

    lax.fori_loop(1, half, take_back, 0)

    def unpack(i, c):
        p = position[i]
        out[i] = back[p // (half * cap), (p // cap) % half, p % cap]
        return c

    lax.fori_loop(0, out.shape[0], unpack, 0, unroll=4)

    def finish(j, c):
        to = lax.rem(mine + j, half)
        tag_copy(to, mine).wait_send()
        left_copy(to, mine).wait_send()
        for kind in range(2):
            psi_copy(kind, to, mine).wait_send()
            ret_copy(kind, to, mine).wait_send()
        return c

    lax.fori_loop(1, half, finish, 0)
    for k in range(2):
        mirror_copy(k).wait_send()


def route(source, position, tags, psi, left, right, n, cap, lsec):
    half = n // 2
    blocks, bl, br = psi.shape
    rsec = right.shape[0]
    slots = (2, half, cap, bl, br)
    vmem, smem = pl.BlockSpec(memory_space=pltpu.VMEM), pl.BlockSpec(memory_space=pltpu.SMEM)
    dma = pltpu.SemaphoreType.DMA
    return pl.pallas_call(
        functools.partial(route_kernel, n, lsec),
        out_shape=jax.ShapeDtypeStruct(psi.shape, jnp.bfloat16),
        in_specs=[smem, smem, vmem, vmem, vmem, pl.BlockSpec(memory_space=pl.ANY)],
        out_specs=vmem,
        scratch_shapes=[
            pltpu.VMEM(slots, jnp.bfloat16),
            pltpu.VMEM(slots, jnp.bfloat16),
            pltpu.VMEM(slots, jnp.bfloat16),
            pltpu.VMEM(slots[1:], F32),
            pltpu.VMEM(right.shape, jnp.bfloat16),
            pltpu.VMEM((rsec, br, br), jnp.bfloat16),
            pltpu.VMEM((rsec, br, br), jnp.bfloat16),
            pltpu.VMEM((half,) + left.shape, jnp.bfloat16),
            pltpu.VMEM(tags.shape, jnp.int32),
            pltpu.SMEM(tags.shape, jnp.int32),
            dma((2, half)), dma((2, half)), dma((2, half)), dma((2, half)),
            dma((half,)), dma((half,)), dma((half,)), dma((half,)),
            dma((2,)), dma((2,)), dma((3,)), dma,
        ],
        compiler_params=pltpu.CompilerParams(
            collective_id=0, has_side_effects=True, vmem_limit_bytes=56 * 1024 * 1024
        ),
        cost_estimate=pl.CostEstimate(
            flops=2 * n * cap * bl * br * (3 * bl + 2 * br),
            bytes_accessed=4 * psi.size + 2 * left.size + 2 * right.size,
            transcendentals=0,
        ),
    )(source, position, tags, psi, left, right)


def shards(psi, block_rows, owner, left_sector, right_sector, left_env, right_env):
    blocks, bl, br = psi.shape
    n = lax.axis_size("sec")
    half = n // 2
    cap = max(2, 2 * blocks // n)
    lsec = left_env.shape[0]
    mine = lax.axis_index("sec") // half
    target = owner[:, 0]
    order = jnp.arange(blocks, dtype=jnp.int32)
    same = target[:, None] == target[None, :]
    earlier = order[None, :] < order[:, None]
    slot = jnp.sum(jnp.where(same & earlier, 1, 0), axis=1).astype(jnp.int32)
    kind = jnp.where(target // half == mine, 0, 1)
    position = (kind * half + target % half) * cap + slot
    slots_all = jnp.arange(n * cap, dtype=jnp.int32)
    match = position[None, :] == slots_all[:, None]
    tag = (right_sector * lsec + left_sector) * (bl + 1) + block_rows
    source = jnp.sum(jnp.where(match, order[None, :], 0), axis=1)
    tags = jnp.sum(jnp.where(match, tag[None, :], 0), axis=1)
    tags = tags.reshape(2, half, cap).transpose(1, 0, 2).reshape(half, 1, 2 * cap)
    tags = jnp.pad(tags, ((0, 0), (0, 0), (0, -(2 * cap) % 128)))
    left = left_env.reshape(lsec, 3 * bl, bl)
    left = jnp.concatenate([left[:, :3 * bl // 2], left[:, 3 * bl // 2:]], axis=2)
    return route(source, position, tags, psi, left, right_env, n, cap, lsec)


def solution(mesh):
    return jax.shard_map(
        shards,
        mesh=mesh,
        in_specs=(
            P(("groups", "sec"), None, None),
            P(("groups", "sec")),
            P(("groups", "sec"), None),
            P(("groups", "sec")),
            P(("groups", "sec")),
            P(("groups", "sec"), None, None, None),
            P(("groups", "sec"), None, None, None),
        ),
        out_specs=P(("groups", "sec"), None, None),
        check_vma=False,
    )
```

time: 444 us -> 165 us (0.37)
  the two profiles are of different devices: /device:TPU:15 before, /device:TPU:0 now
where the time goes in v2:
time: 165 us; the launch traced here: 164 us
  Pallas kernels  156 us (95%)
  local copies, waits for them, and re-layouts  4.82 us (3%)
  other arithmetic  3.09 us (2%)
    pallas_call x1, Pallas kernels, route(): pl.pallas_call(functools.partial(route_kernel, n, lsec), out_shape=jax.Sh...  156 us

profile of v2, /device:TPU:0, one launch (start us, length us, event | category | flops | bytes accessed | tf_op | source)
XLA Modules:
  0.0 164.4 jit_solution(9105766618003385968)
XLA Ops:
  0.0 0.9 select_reduce_fusion.2
  0.9 0.7 multiply_add_fusion
  1.6 0.0 copy-start
  1.6 0.7 select_reduce_fusion
  2.4 0.1 reshape.67
  2.5 0.1 reshape.68
  2.5 0.6 pad.4.tags_in
  3.1 1.0 fusion.3
  4.1 0.7 pad_maximum_fusion.left_in
  4.9 0.0 copy-done
  4.9 156.4 %shard_map.73 = bf16[128,64,128]{2,1,0:T(8,128)(2,1)} custom-call(s32[256]{0:T(256)} %get-tuple-element.6.source, s32[128]{0:T(128)} %copy-done, s32[8,1,128]{2,1,0:T(1,128)} %pad.4.tags_in, bf16[128,64,128]{2,1,0:T(8,128)(2,1)} %psi.1, bf16[4,96,128]{2,1,0:T(8,128)(2,1)} %pad_maximum_fusion.left_in, bf16[32,2,128,128]{3,2,1,0:T(8,128)(2,1)} %right_in.1), custom_call_target="tpu_custom_call" | custom-call | flops 1879048192 | bytes 6389760 | tf_op jit(solution)/shard_map/pallas_call | solution.py:235
  161.3 3.1 %copy.11 = bf16[128,64,128]{2,1,0:T(8,128)(2,1)} copy(bf16[128,64,128]{2,1,0:T(8,128)(2,1)} %shard_map.73) | data formatting | bytes 4194304
  (1 shorter events, 0.0 us)
Async XLA Ops:
  1.6 3.2 %copy-start = (s32[128]{0:T(128)}, s32[128]{0:T(128)S(1)}, u32[]{:S(2)}) copy-start(s32[128]{0:T(128)S(1)} %get-tuple-element.10.position) | copy-start | bytes 1540

commit v3 on v0

v3 whole, which is shorter than its diff:
```python
import functools

import jax
import jax.numpy as jnp
from jax import lax
from jax.experimental import pallas as pl
from jax.experimental.pallas import tpu as pltpu
from jax.sharding import PartitionSpec as P

F32 = jnp.float32
PLANES = 4
CHUNKS = 8


def route_kernel(
    n, lsec,
    source, position, tags_in, psi, left_in, right_in,
    out,
    sent, got, back, passed, right0, right1, right2, right3, left_p, left_f, tags_v, tags_w, tags_p, tags_f,
    psi_send, psi_recv, ret_send, ret_recv, pass_send, pass_recv, tag_send, tag_recv, tagf_send, tagf_recv,
    left_send, left_recv, leftf_send, leftf_recv, up_send, up_recv, r_send, r_recv, own_sem, self_sem, tag_sem,
):
    plane = n // PLANES
    cap, bl, br = sent.shape[2:]
    rsec = right0.shape[0]
    piece = rsec // CHUNKS
    me = lax.axis_index("sec")
    level = me // plane
    first = level * plane
    mine = me - first
    outer = (level == 0) | (level == PLANES - 1)
    upper = level >= PLANES // 2
    inward = jnp.where(upper, me - plane, me + plane)
    outward = jnp.where(upper, me + plane, me - plane)
    rights = (right0, right1, right2, right3)
    order = (1, 2, 0, 3)

    barrier = pltpu.get_barrier_semaphore()

    def greet(j, c):
        pl.semaphore_signal(barrier, inc=1, device_id={"sec": first + lax.rem(mine + j, plane)})
        return c

    lax.fori_loop(1, plane, greet, 0)
    pl.semaphore_signal(barrier, inc=1, device_id={"sec": inward})

    @pl.when(jnp.logical_not(outer))
    def _():
        pl.semaphore_signal(barrier, inc=1, device_id={"sec": outward})
        pl.semaphore_wait(barrier, plane + 1)

    @pl.when(outer)
    def _():
        pl.semaphore_wait(barrier, plane)

    def remote(src, dst, send, recv, to):
        return pltpu.make_async_remote_copy(
            src_ref=src, dst_ref=dst, send_sem=send, recv_sem=recv, device_id={"sec": to}
        )

    def chunk_copy(src, kind, as_kind, q, to):
        part = pl.ds(q * piece, piece)
        return remote(src.at[part], rights[as_kind].at[part], r_send.at[kind, q], r_recv.at[as_kind, q], to)

    def tag_copy(to, slot):
        return remote(tags_in.at[to], tags_v.at[slot], tag_send.at[to], tag_recv.at[slot], first + to)

    def left_copy(to, slot):
        return remote(left_in, left_p.at[slot], left_send.at[to], left_recv.at[slot], first + to)

    def psi_copy(kind, to, slot):
        return remote(
            sent.at[kind, to], got.at[kind, slot], psi_send.at[kind, to], psi_recv.at[kind, slot], first + to
        )

    def ret_copy(src, kind, to, slot):
        return remote(src, back.at[kind, slot], ret_send.at[kind, to], ret_recv.at[kind, slot], first + to)

    def tagf_copy(s):
        return remote(tags_v.at[s], tags_w.at[s], tagf_send.at[s], tagf_recv.at[s], inward)

    def pass_in(kind, s):
        return remote(
            got.at[kind, s], passed.at[kind - 1, s], pass_send.at[kind - 1, s], pass_recv.at[kind - 1, s], inward
        )

    def pass_back(kind, s):
        return remote(
            passed.at[kind - 1, s], passed.at[kind - 1, s], pass_send.at[kind - 1, s],
            pass_recv.at[kind - 1, s], outward,
        )

    def up_copy():
        return remote(left_in, left_f.at[mine], up_send, up_recv, inward)

    def leftf_copy(to, slot):
        return remote(left_f.at[mine], left_f.at[slot], leftf_send.at[to], leftf_recv.at[slot], first + to)

    def each(work, low=0):
        def one(j, c):
            work(lax.rem(mine + j, plane))
            return c
        lax.fori_loop(low, plane, one, 0)

    def each_from(work, low=0):
        def one(j, c):
            work(lax.rem(mine + plane - j, plane))
            return c
        lax.fori_loop(low, plane, one, 0)

    def start_right(kind, as_kind, to):
        def one(q, c):
            chunk_copy(right_in, kind, as_kind, q, to).start()
            return c
        lax.fori_loop(0, CHUNKS, one, 0)

    def take_right(kind):
        def one(q, c):
            chunk_copy(rights[kind], kind, kind, q, inward).wait_recv()
            return c
        lax.fori_loop(0, CHUNKS, one, 0)

    def end_right(kind, as_kind):
        def one(q, c):
            chunk_copy(right_in, kind, as_kind, q, inward).wait_send()
            return c
        lax.fori_loop(0, CHUNKS, one, 0)

    own_left = pltpu.make_async_copy(left_in, left_p.at[mine], own_sem.at[1])
    own_tags = pltpu.make_async_copy(tags_in.at[mine], tags_v.at[mine], own_sem.at[2])
    own_left.start()
    own_tags.start()

    @pl.when(outer)
    def _():
        start_right(0, 0, inward)
        up_copy().start()

    @pl.when(jnp.logical_not(outer))
    def _():
        start_right(1, 2, inward)

    def send_small(to):
        tag_copy(to, mine).start()
        left_copy(to, mine).start()

    each(send_small, 1)

    def pack(kind, dest, into):
        def one(s, c):
            into[kind, dest, s] = psi[source[(kind * plane + dest) * cap + s]]
            return c
        lax.fori_loop(0, cap, one, 0, unroll=min(cap, 4))

    for kind in order:
        def send_psi(to):
            pack(kind, to, sent)
            psi_copy(kind, to, mine).start()
        each(send_psi, 1)
        pack(kind, mine, got)
    own_tags.wait()
    own_left.wait()

    group = min(cap, 8)
    line = lax.broadcasted_iota(jnp.int32, (bl, br), 0)

    def serve(table, left, blocks, index, kind, src, into, slot):
        def fields(s):
            tag = table[src, 0, kind * cap + s]
            return tag % (bl + 1), (tag // (bl + 1)) % lsec, tag // ((bl + 1) * lsec)

        def one(g, c):
            slots = [g * group + i for i in range(group)]
            parts = []
            for s in slots:
                rows, lsel, _ = fields(s)
                block = jnp.where(line < rows, blocks[index, src, s], jnp.zeros((), jnp.bfloat16))
                packed = left[src, lsel]
                parts.append(jnp.concatenate([
                    jnp.dot(packed[:, :bl], block, preferred_element_type=F32),
                    jnp.dot(packed[:, bl:], block, preferred_element_type=F32),
                ], axis=0))
            for s, made in zip(slots, parts):
                rows, _, rsel = fields(s)
                far = made[:bl]
                for k in range(2):
                    moved = made[(k + 1) * bl:(k + 2) * bl].astype(jnp.bfloat16)
                    far = far + jnp.dot(moved, rights[kind][rsel, k], preferred_element_type=F32)
                into[slot, src, s] = jnp.where(line < rows, far, 0.0).astype(jnp.bfloat16)
            return c

        lax.fori_loop(0, cap // group, one, 0)

    def serve_plane(kind, src):
        @pl.when(src != mine)
        def _():
            psi_copy(kind, src, src).wait_recv()
            serve(tags_p, left_p, got, kind, kind, src, got, kind)
            ret_copy(got.at[kind, src], kind, src, mine).start()

        @pl.when(src == mine)
        def _():
            serve(tags_p, left_p, got, kind, kind, src, back, kind)

    def take_left(src):
        left_copy(src, src).wait_recv()

    def take_tags(src):
        tag_copy(src, src).wait_recv()

    def to_smem(values, table):
        copy = pltpu.make_async_copy(values, table, tag_sem)
        copy.start()
        copy.wait()

    @pl.when(outer)
    def _():
        own = pltpu.make_async_copy(right_in, right0, own_sem.at[0])
        own.start()
        each_from(take_tags, 1)
        each_from(lambda s: tagf_copy(s).start())
        for kind in (1, 2):
            pass_in(kind, mine).start()

            def forward(src):
                psi_copy(kind, src, src).wait_recv()
                pass_in(kind, src).start()
            each_from(forward, 1)
        to_smem(tags_v, tags_p)
        each_from(take_left, 1)
        own.wait()
        each_from(lambda src: serve_plane(0, src))

        def bring(kind, src):
            pass_back(kind, src).wait_recv()

            @pl.when(src != mine)
            def _():
                ret_copy(passed.at[kind - 1, src], kind, src, mine).start()

            @pl.when(src == mine)
            def _():
                pltpu.make_async_copy(passed.at[kind - 1, src], back.at[kind, src], self_sem.at[kind - 1]).start()

        for kind in (1, 2):
            each_from(lambda src: bring(kind, src))
        take_right(3)
        each_from(lambda src: serve_plane(3, src))
        for kind in (1, 2):
            pltpu.make_async_copy(passed.at[kind - 1, mine], back.at[kind, mine], self_sem.at[kind - 1]).wait()

    @pl.when(jnp.logical_not(outer))
    def _():
        own = pltpu.make_async_copy(right_in, right1, own_sem.at[0])
        own.start()
        up_copy().wait_recv()
        each(lambda to: leftf_copy(to, mine).start(), 1)
        each_from(take_tags, 1)
        to_smem(tags_v, tags_p)
        each_from(take_left, 1)
        own.wait()

        def relay_out(q):
            chunk = chunk_copy(right0, 0, 3, q, inward)
            chunk_copy(right0, 0, 0, q, inward).wait_recv()
            chunk.start()

        def relay_back(q):
            chunk_copy(right3, 3, 3, q, outward).wait_recv()
            chunk_copy(right3, 3, 3, q, outward).start()

        def serve_passed(kind, src):
            pass_in(kind, src).wait_recv()
            serve(tags_f, left_f, passed, kind - 1, kind, src, passed, kind - 1)
            pass_back(kind, src).start()

        steps = CHUNKS // 2
        share = plane // steps

        def early(work):
            def some(q):
                def one(i, c):
                    work(lax.rem(mine + plane - (q * share + i), plane))
                    return c
                lax.fori_loop(0, share, one, 0)
            return some

        def phase(low, work):
            def one(q, c):
                relay_out(q + low)

                @pl.when(q + low > 0)
                def _():
                    relay_back(q + low - 1)
                work(q)
                return c
            lax.fori_loop(0, steps, one, 0)

        phase(0, early(lambda src: serve_plane(1, src)))
        each_from(lambda s: tagf_copy(s).wait_recv())
        to_smem(tags_w, tags_f)
        each_from(lambda src: leftf_copy(src, src).wait_recv(), 1)
        phase(steps, early(lambda src: serve_passed(1, src)))
        relay_back(CHUNKS - 1)
        take_right(2)
        each_from(lambda src: serve_passed(2, src))
        each_from(lambda src: serve_plane(2, src))
        each_from(lambda src: serve_plane(0, src))
        each_from(lambda src: serve_plane(3, src))

    for kind in order:
        each_from(lambda src: ret_copy(back.at[kind, src], kind, src, src).wait_recv(), 1)

    def unpack(i, c):
        p = position[i]
        out[i] = back[p // (plane * cap), (p // cap) % plane, p % cap]
        return c

    lax.fori_loop(0, out.shape[0], unpack, 0, unroll=4)

    def finish(to):
        tag_copy(to, mine).wait_send()
        left_copy(to, mine).wait_send()
        for kind in range(4):
            psi_copy(kind, to, mine).wait_send()
            ret_copy(got.at[kind, to], kind, to, mine).wait_send()

    each(finish, 1)

    @pl.when(outer)
    def _():
        end_right(0, 0)
        up_copy().wait_send()
        each(lambda s: tagf_copy(s).wait_send())
        for kind in (1, 2):
            each(lambda s: pass_in(kind, s).wait_send())

    @pl.when(jnp.logical_not(outer))
    def _():
        end_right(1, 2)
        end_right(0, 3)
        end_right(3, 3)
        each(lambda to: leftf_copy(to, mine).wait_send(), 1)
        for kind in (1, 2):
            each(lambda s: pass_back(kind, s).wait_send())


def route(source, position, tags, psi, left, right, n, cap, lsec):
    plane = n // PLANES
    blocks, bl, br = psi.shape
    slots = (4, plane, cap, bl, br)
    vmem, smem = pl.BlockSpec(memory_space=pltpu.VMEM), pl.BlockSpec(memory_space=pltpu.SMEM)
    dma = pltpu.SemaphoreType.DMA
    return pl.pallas_call(
        functools.partial(route_kernel, n, lsec),
        out_shape=jax.ShapeDtypeStruct(psi.shape, jnp.bfloat16),
        in_specs=[smem, smem, vmem, vmem, vmem, pl.BlockSpec(memory_space=pl.ANY)],
        out_specs=vmem,
        scratch_shapes=[
            pltpu.VMEM(slots, jnp.bfloat16),
            pltpu.VMEM(slots, jnp.bfloat16),
            pltpu.VMEM(slots, jnp.bfloat16),
            pltpu.VMEM((2,) + slots[1:], jnp.bfloat16),
            pltpu.VMEM(right.shape, jnp.bfloat16),
            pltpu.VMEM(right.shape, jnp.bfloat16),
            pltpu.VMEM(right.shape, jnp.bfloat16),
            pltpu.VMEM(right.shape, jnp.bfloat16),
            pltpu.VMEM((plane,) + left.shape, jnp.bfloat16),
            pltpu.VMEM((plane,) + left.shape, jnp.bfloat16),
            pltpu.VMEM(tags.shape, jnp.int32),
            pltpu.VMEM(tags.shape, jnp.int32),
            pltpu.SMEM(tags.shape, jnp.int32),
            pltpu.SMEM(tags.shape, jnp.int32),
            dma((4, plane)), dma((4, plane)), dma((4, plane)), dma((4, plane)),
            dma((2, plane)), dma((2, plane)),
            dma((plane,)), dma((plane,)), dma((plane,)), dma((plane,)),
            dma((plane,)), dma((plane,)), dma((plane,)), dma((plane,)),
            dma, dma, dma((4, CHUNKS)), dma((4, CHUNKS)), dma((3,)), dma((2,)), dma,
        ],
        compiler_params=pltpu.CompilerParams(
            collective_id=0, has_side_effects=True, vmem_limit_bytes=56 * 1024 * 1024
        ),
        cost_estimate=pl.CostEstimate(
            flops=2 * n * cap * bl * br * (3 * bl + 2 * br),
            bytes_accessed=4 * psi.size + 2 * left.size + 2 * right.size,
            transcendentals=0,
        ),
    )(source, position, tags, psi, left, right)


def shards(psi, block_rows, owner, left_sector, right_sector, left_env, right_env):
    blocks, bl, br = psi.shape
    n = lax.axis_size("sec")
    plane = n // PLANES
    cap = max(2, 2 * blocks // n)
    lsec = left_env.shape[0]
    upper = lax.axis_index("sec") // plane >= PLANES // 2
    target = owner[:, 0]
    order = jnp.arange(blocks, dtype=jnp.int32)
    same = target[:, None] == target[None, :]
    earlier = order[None, :] < order[:, None]
    slot = jnp.sum(jnp.where(same & earlier, 1, 0), axis=1).astype(jnp.int32)
    level = target // plane
    kind = jnp.where(upper, PLANES - 1 - level, level)
    position = (kind * plane + target % plane) * cap + slot
    slots_all = jnp.arange(n * cap, dtype=jnp.int32)
    match = position[None, :] == slots_all[:, None]
    tag = (right_sector * lsec + left_sector) * (bl + 1) + block_rows
    source = jnp.sum(jnp.where(match, order[None, :], 0), axis=1)
    tags = jnp.sum(jnp.where(match, tag[None, :], 0), axis=1)
    tags = tags.reshape(4, plane, cap).transpose(1, 0, 2).reshape(plane, 1, 4 * cap)
    tags = jnp.pad(tags, ((0, 0), (0, 0), (0, -(4 * cap) % 128)))
    left = left_env.reshape(lsec, 3 * bl, bl)
    left = jnp.concatenate([left[:, :3 * bl // 2], left[:, 3 * bl // 2:]], axis=2)
    return route(source, position, tags, psi, left, right_env, n, cap, lsec)


def solution(mesh):
    return jax.shard_map(
        shards,
        mesh=mesh,
        in_specs=(
            P(("groups", "sec"), None, None),
            P(("groups", "sec")),
            P(("groups", "sec"), None),
            P(("groups", "sec")),
            P(("groups", "sec")),
            P(("groups", "sec"), None, None, None),
            P(("groups", "sec"), None, None, None),
        ),
        out_specs=P(("groups", "sec"), None, None),
        check_vma=False,
    )
```

time: 444 us -> 183 us (0.41)
  the two profiles are of different devices: /device:TPU:15 before, /device:TPU:0 now
where the time goes in v3:
time: 183 us
  Pallas kernels  175 us (96%)
  local copies, waits for them, and re-layouts  4.82 us (3%)
  other arithmetic  3.1 us (2%)
    pallas_call x1, Pallas kernels, route(): pl.pallas_call(functools.partial(route_kernel, n, lsec), out_shape=jax.Sh...  175 us

profile of v3, /device:TPU:0, one launch (start us, length us, event | category | flops | bytes accessed | tf_op | source)
XLA Modules:
  0.0 182.9 jit_solution(8933030511779397325)
XLA Ops:
  0.0 0.9 select_reduce_fusion.2
  0.9 0.7 multiply_add_fusion
  1.6 0.0 copy-start
  1.6 0.7 select_reduce_fusion
  2.4 0.1 reshape.67
  2.5 0.1 reshape.68
  2.5 0.6 pad.4.tags_in
  3.2 1.0 fusion.3
  4.1 0.7 pad_maximum_fusion.left_in
  4.9 0.0 copy-done
  4.9 175.0 %shard_map.73 = bf16[128,64,128]{2,1,0:T(8,128)(2,1)} custom-call(s32[256]{0:T(256)} %get-tuple-element.6.source, s32[128]{0:T(128)} %copy-done, s32[4,1,128]{2,1,0:T(1,128)} %pad.4.tags_in, bf16[128,64,128]{2,1,0:T(8,128)(2,1)} %psi.1, bf16[4,96,128]{2,1,0:T(8,128)(2,1)} %pad_maximum_fusion.left_in, bf16[32,2,128,128]{3,2,1,0:T(8,128)(2,1)} %right_in.1), custom_call_target="tpu_custom_call" | custom-call | flops 1879048192 | bytes 6389760 | tf_op jit(solution)/shard_map/pallas_call | solution.py:354
  179.9 3.1 %copy.11 = bf16[128,64,128]{2,1,0:T(8,128)(2,1)} copy(bf16[128,64,128]{2,1,0:T(8,128)(2,1)} %shard_map.73) | data formatting | bytes 4194304
  (1 shorter events, 0.0 us)
Async XLA Ops:
  1.6 3.2 %copy-start = (s32[128]{0:T(128)}, s32[128]{0:T(128)S(1)}, u32[]{:S(2)}) copy-start(s32[128]{0:T(128)S(1)} %get-tuple-element.10.position) | copy-start | bytes 1540

commit v4 on v2

--- a/solution.py
+++ b/solution.py
@@ -24,6 +24,9 @@
     first = (me // half) * half
     mine = me - first
     partner = lax.rem(me + half, n)
+    quarter = half // 2
+    corner = (mine // quarter) * quarter
+    across = lax.rem(mine + quarter, half)
 
     barrier = pltpu.get_barrier_semaphore()
 
@@ -49,11 +52,14 @@
             recv_sem=tag_recv.at[slot], device_id={"sec": first + to},
         )
 
-    def left_copy(to, slot):
-        return pltpu.make_async_remote_copy(
-            src_ref=left_in, dst_ref=left.at[slot], send_sem=left_send.at[to],
+    def left_copy(src, to, slot, sem):
+        return pltpu.make_async_remote_copy(
+            src_ref=src, dst_ref=left.at[slot], send_sem=left_send.at[sem, to],
             recv_sem=left_recv.at[slot], device_id={"sec": first + to},
         )
+
+    def beside(j):
+        return corner + lax.rem(mine - corner + j, quarter)
 
     def psi_copy(kind, to, slot):
         return pltpu.make_async_remote_copy(
@@ -80,10 +86,19 @@
     def send_small(j, c):
         to = lax.rem(mine + j, half)
         tag_copy(to, mine).start()
-        left_copy(to, mine).start()
-        return c
-
+        return c
+
+    def send_left(j, c):
+        left_copy(left_in, beside(j), mine, 0).start()
+        return c
+
+    def hand_left(j, c):
+        left_copy(left.at[across], beside(j), across, 1).start()
+        return c
+
+    left_copy(left_in, across, mine, 0).start()
     lax.fori_loop(1, half, send_small, 0)
+    lax.fori_loop(1, quarter, send_left, 0)
 
     def pack(kind, dest, into):
         def one(s, c):
@@ -100,16 +115,26 @@
         lax.fori_loop(1, half, send_psi, 0)
         pack(kind, mine, got)
 
+    left_copy(left_in, across, across, 0).wait_recv()
+    lax.fori_loop(1, quarter, hand_left, 0)
+
     for copy in own:
         copy.wait()
 
     def take_small(j, c):
         src = lax.rem(mine + half - j, half)
         tag_copy(src, src).wait_recv()
-        left_copy(src, src).wait_recv()
+        return c
+
+    def take_left(j, c):
+        src = beside(j)
+        left_copy(left_in, src, src, 0).wait_recv()
+        src = lax.rem(src + quarter, half)
+        left_copy(left_in, src, src, 0).wait_recv()
         return c
 
     lax.fori_loop(1, half, take_small, 0)
+    lax.fori_loop(1, quarter, take_left, 0)
     copy = pltpu.make_async_copy(tags_v, tags, tag_sem)
     copy.start()
     copy.wait()
@@ -214,13 +239,19 @@
     def finish(j, c):
         to = lax.rem(mine + j, half)
         tag_copy(to, mine).wait_send()
-        left_copy(to, mine).wait_send()
         for kind in range(2):
             psi_copy(kind, to, mine).wait_send()
             ret_copy(kind, to, mine).wait_send()
         return c
 
+    def finish_left(j, c):
+        left_copy(left_in, beside(j), mine, 0).wait_send()
+        left_copy(left_in, beside(j), across, 1).wait_send()
+        return c
+
     lax.fori_loop(1, half, finish, 0)
+    lax.fori_loop(1, quarter, finish_left, 0)
+    left_copy(left_in, across, mine, 0).wait_send()
     for k in range(2):
         mirror_copy(k).wait_send()
 
@@ -249,7 +280,7 @@
             pltpu.VMEM(tags.shape, jnp.int32),
             pltpu.SMEM(tags.shape, jnp.int32),
             dma((2, half)), dma((2, half)), dma((2, half)), dma((2, half)),
-            dma((half,)), dma((half,)), dma((half,)), dma((half,)),
+            dma((half,)), dma((half,)), dma((2, half)), dma((half,)),
             dma((2,)), dma((2,)), dma((3,)), dma,
         ],
         compiler_params=pltpu.CompilerParams(

time: 165 us -> 158 us (0.958)
  Pallas kernels: 156 us -> 150 us
    pallas_call x1, Pallas kernels: 156 us -> 150 us  [route(): pl.pallas_call(functools.partial(route_kernel, n, lsec), out_shape=jax.Sh...]
where the time goes in v4:
time: 158 us
  Pallas kernels  150 us (95%)
  local copies, waits for them, and re-layouts  4.82 us (3%)
  other arithmetic  3.09 us (2%)
    pallas_call x1, Pallas kernels, route(): pl.pallas_call(functools.partial(route_kernel, n, lsec), out_shape=jax.Sh...  150 us

profile of v4, /device:TPU:0, one launch (start us, length us, event | category | flops | bytes accessed | tf_op | source)
XLA Modules:
  0.0 158.1 jit_solution(8370076351850989415)
XLA Ops:
  0.0 0.9 select_reduce_fusion.2
  0.9 0.7 multiply_add_fusion
  1.6 0.0 copy-start
  1.6 0.7 select_reduce_fusion
  2.4 0.1 reshape.67
  2.5 0.1 reshape.68
  2.5 0.6 pad.4.tags_in
  3.1 1.0 fusion.3
  4.1 0.7 pad_maximum_fusion.left_in
  4.9 0.0 copy-done
  4.9 150.2 %shard_map.73 = bf16[128,64,128]{2,1,0:T(8,128)(2,1)} custom-call(s32[256]{0:T(256)} %get-tuple-element.6.source, s32[128]{0:T(128)} %copy-done, s32[8,1,128]{2,1,0:T(1,128)} %pad.4.tags_in, bf16[128,64,128]{2,1,0:T(8,128)(2,1)} %psi.1, bf16[4,96,128]{2,1,0:T(8,128)(2,1)} %pad_maximum_fusion.left_in, bf16[32,2,128,128]{3,2,1,0:T(8,128)(2,1)} %right_in.1), custom_call_target="tpu_custom_call" | custom-call | flops 1879048192 | bytes 6389760 | tf_op jit(solution)/shard_map/pallas_call | solution.py:266
  155.0 3.1 %copy.11 = bf16[128,64,128]{2,1,0:T(8,128)(2,1)} copy(bf16[128,64,128]{2,1,0:T(8,128)(2,1)} %shard_map.73) | data formatting | bytes 4194304
  (1 shorter events, 0.0 us)
Async XLA Ops:
  1.6 3.2 %copy-start = (s32[128]{0:T(128)}, s32[128]{0:T(128)S(1)}, u32[]{:S(2)}) copy-start(s32[128]{0:T(128)S(1)} %get-tuple-element.10.position) | copy-start | bytes 1540

commit v5 on v4

--- a/solution.py
+++ b/solution.py
@@ -8,15 +8,16 @@
 from jax.sharding import PartitionSpec as P
 
 F32 = jnp.float32
+PIECES = 4
 
 
 def route_kernel(
     n, lsec,
     source, position, tags_in, psi, left_in, right_in,
     out,
-    sent, got, back, total, right, mirror0, mirror1, left, tags_v, tags,
+    sent, got, back, total, right, mirror0, mirror1, near0, near1, left, tags_v, tags,
     psi_send, psi_recv, ret_send, ret_recv, tag_send, tag_recv, left_send, left_recv,
-    mir_send, mir_recv, own_sem, tag_sem,
+    mir_send, mir_recv, hop_send, hop_recv, own_sem, tag_sem,
 ):
     half = n // 2
     cap, bl, br = sent.shape[2:]
@@ -27,6 +28,9 @@
     quarter = half // 2
     corner = (mine // quarter) * quarter
     across = lax.rem(mine + quarter, half)
+    outer = (first == 0) == (corner == 0)
+    facing = lax.rem(first + across + half, n)
+    piece = right_in.shape[0] // PIECES
 
     barrier = pltpu.get_barrier_semaphore()
 
@@ -36,15 +40,45 @@
 
     lax.fori_loop(1, half, greet, 0)
     pl.semaphore_signal(barrier, inc=1, device_id={"sec": partner})
-    pl.semaphore_wait(barrier, half)
-
-    mirrors = (mirror0, mirror1)
-
-    def mirror_copy(k):
-        return pltpu.make_async_remote_copy(
-            src_ref=right_in.at[:, k], dst_ref=mirrors[k], send_sem=mir_send.at[k],
-            recv_sem=mir_recv.at[k], device_id={"sec": partner},
-        )
+
+    @pl.when(outer)
+    def _():
+        pl.semaphore_wait(barrier, half)
+
+    @pl.when(jnp.logical_not(outer))
+    def _():
+        pl.semaphore_signal(barrier, inc=1, device_id={"sec": facing})
+        pl.semaphore_wait(barrier, half + 1)
+
+    mirrors, nears = (mirror0, mirror1), (near0, near1)
+
+    def mirror_copy(k, q):
+        part = pl.ds(q * piece, piece)
+        return pltpu.make_async_remote_copy(
+            src_ref=right_in.at[part, k], dst_ref=mirrors[k].at[part], send_sem=mir_send.at[k, q],
+            recv_sem=mir_recv.at[k, q], device_id={"sec": partner},
+        )
+
+    def hop_copy(k, q):
+        part = pl.ds(q * piece, piece)
+        return pltpu.make_async_remote_copy(
+            src_ref=right_in.at[part, k], dst_ref=nears[k].at[part], send_sem=hop_send.at[k, q],
+            recv_sem=hop_recv.at[k, q], device_id={"sec": first + across},
+        )
+
+    def relay_copy(k, q):
+        part = pl.ds(q * piece, piece)
+        return pltpu.make_async_remote_copy(
+            src_ref=nears[k].at[part], dst_ref=mirrors[k].at[part], send_sem=hop_send.at[k, q],
+            recv_sem=mir_recv.at[k, q], device_id={"sec": facing},
+        )
+
+    def pieces(work):
+        for k in range(2):
+            def one(q, c):
+                work(k, q)
+                return c
+            lax.fori_loop(0, PIECES, one, 0)
 
     def tag_copy(to, slot):
         return pltpu.make_async_remote_copy(
@@ -67,14 +101,32 @@
             recv_sem=psi_recv.at[kind, slot], device_id={"sec": first + to},
         )
 
+    def aside_copy(to, at, slot):
+        return pltpu.make_async_remote_copy(
+            src_ref=sent.at[0, to], dst_ref=got.at[2, slot], send_sem=psi_send.at[0, to],
+            recv_sem=psi_recv.at[2, slot], device_id={"sec": first + at},
+        )
+
+    def aside_ret(to, slot):
+        return pltpu.make_async_remote_copy(
+            src_ref=got.at[2, to], dst_ref=back.at[0, slot], send_sem=ret_send.at[2, to],
+            recv_sem=ret_recv.at[0, slot], device_id={"sec": first + to},
+        )
+
     def ret_copy(kind, to, slot):
         return pltpu.make_async_remote_copy(
             src_ref=got.at[kind, to], dst_ref=back.at[kind, slot], send_sem=ret_send.at[kind, to],
             recv_sem=ret_recv.at[kind, slot], device_id={"sec": first + to},
         )
 
-    mirror_copy(0).start()
-    mirror_copy(1).start()
+    @pl.when(outer)
+    def _():
+        pieces(lambda k, q: hop_copy(k, q).start())
+
+    @pl.when(jnp.logical_not(outer))
+    def _():
+        pieces(lambda k, q: mirror_copy(k, q).start())
+
     own = [
         pltpu.make_async_copy(right_in, right, own_sem.at[0]),
         pltpu.make_async_copy(left_in, left.at[mine], own_sem.at[1]),
@@ -100,17 +152,34 @@
     lax.fori_loop(1, half, send_small, 0)
     lax.fori_loop(1, quarter, send_left, 0)
 
-    def pack(kind, dest, into):
+    def pack(kind, dest, into, at_kind=None, at=None):
+        at_kind, at = (kind, dest) if at is None else (at_kind, at)
+
         def one(s, c):
-            into[kind, dest, s] = psi[source[(kind * half + dest) * cap + s]]
+            into[at_kind, at, s] = psi[source[(kind * half + dest) * cap + s]]
             return c
         lax.fori_loop(0, cap, one, 0, unroll=min(cap, 4))
 
     for kind in range(2):
         def send_psi(j, c):
             to = lax.rem(mine + j, half)
-            pack(kind, to, sent)
-            psi_copy(kind, to, mine).start()
+            aside = jnp.logical_not(outer) & (to // quarter != mine // quarter) & (kind == 0)
+            at = lax.rem(to + quarter, half)
+
+            @pl.when(jnp.logical_not(aside))
+            def _():
+                pack(kind, to, sent)
+                psi_copy(kind, to, mine).start()
+
+            if kind == 0:
+                @pl.when(aside & (at != mine))
+                def _():
+                    pack(0, to, sent)
+                    aside_copy(to, at, mine).start()
+
+                @pl.when(aside & (at == mine))
+                def _():
+                    pack(0, to, got, 2, mine)
             return c
         lax.fori_loop(1, half, send_psi, 0)
         pack(kind, mine, got)
@@ -162,14 +231,15 @@
             return c
         lax.fori_loop(0, cap // group, one, 0)
 
-    def whole(kind, src, into):
+    def whole(kind, src, into, at_kind, at):
         def work(slots):
             parts = [contract_left(kind, src, s) for s in slots]
             for s, (local, m0, m1) in zip(slots, parts):
                 rows, _, rsel = fields(kind, src, s)
-                far = jnp.dot(m0, right[rsel, 0], preferred_element_type=F32)
-                far = far + jnp.dot(m1, right[rsel, 1], preferred_element_type=F32)
-                into[kind, src, s] = jnp.where(line < rows, local + far, 0.0).astype(jnp.bfloat16)
+                r0, r1 = (near0[rsel], near1[rsel]) if kind == 2 else (right[rsel, 0], right[rsel, 1])
+                far = jnp.dot(m0, r0, preferred_element_type=F32)
+                far = far + jnp.dot(m1, r1, preferred_element_type=F32)
+                into[at_kind, at, s] = jnp.where(line < rows, local + far, 0.0).astype(jnp.bfloat16)
         over_groups(work)
 
     def first_term(src):
@@ -189,17 +259,65 @@
                 into[1, src, s] = jnp.where(line < rows, far, 0.0).astype(jnp.bfloat16)
         over_groups(work)
 
-    def serve_near(j, c):
-        src = lax.rem(mine + half - j, half)
+    def serve_near(src):
         psi_copy(0, src, src).wait_recv()
-        whole(0, src, got)
+        whole(0, src, got, 0, src)
         ret_copy(0, src, mine).start()
-        return c
-
-    lax.fori_loop(1, half, serve_near, 0)
-    whole(0, mine, back)
-
-    mirror_copy(0).wait_recv()
+
+    def serve_beside(j, c):
+        serve_near(beside(j))
+        return c
+
+    def serve_aside(j, c):
+        src = beside(j)
+        aside_copy(src, src, src).wait_recv()
+        whole(2, src, got, 2, src)
+        aside_ret(src, across).start()
+        return c
+
+    @pl.when(outer)
+    def _():
+        lax.fori_loop(1, quarter, serve_beside, 0)
+        whole(0, mine, back, 0, mine)
+
+    @pl.when(jnp.logical_not(outer))
+    def _():
+        share = quarter // PIECES
+
+        def relay_and_serve(k):
+            def one(q, c):
+                hop_copy(k, q).wait_recv()
+                relay_copy(k, q).start()
+
+                def some(i, c):
+                    j = q * share + i
+                    if k == 0:
+                        @pl.when(j > 0)
+                        def _():
+                            serve_near(beside(j))
+
+                        @pl.when(j == 0)
+                        def _():
+                            whole(0, mine, back, 0, mine)
+                    else:
+                        serve_near(lax.rem(beside(j) + quarter, half))
+                    return c
+                lax.fori_loop(0, share, some, 0)
+                return c
+            lax.fori_loop(0, PIECES, one, 0)
+
+        relay_and_serve(0)
+        relay_and_serve(1)
+        lax.fori_loop(1, quarter, serve_aside, 0)
+        whole(2, mine, back, 0, across)
+
+    def take_mirror(k):
+        def one(q, c):
+            mirror_copy(k, q).wait_recv()
+            return c
+        lax.fori_loop(0, PIECES, one, 0)
+
+    take_mirror(0)
 
     def begin_far(j, c):
         src = lax.rem(mine + half - j, half)
@@ -210,7 +328,7 @@
     lax.fori_loop(1, half, begin_far, 0)
     first_term(mine)
 
-    mirror_copy(1).wait_recv()
+    take_mirror(1)
 
     def end_far(j, c):
         src = lax.rem(mine + half - j, half)
@@ -223,7 +341,10 @@
 
     def take_back(j, c):
         src = lax.rem(mine + half - j, half)
-        ret_copy(0, src, src).wait_recv()
+
+        @pl.when(outer | (src != across))
+        def _():
+            ret_copy(0, src, src).wait_recv()
         ret_copy(1, src, src).wait_recv()
         return c
 
@@ -239,9 +360,21 @@
     def finish(j, c):
         to = lax.rem(mine + j, half)
         tag_copy(to, mine).wait_send()
-        for kind in range(2):
-            psi_copy(kind, to, mine).wait_send()
-            ret_copy(kind, to, mine).wait_send()
+        near = to // quarter == mine // quarter
+
+        @pl.when(outer | (to != across))
+        def _():
+            psi_copy(0, to, mine).wait_send()
+
+        @pl.when(jnp.logical_not(outer) | near)
+        def _():
+            ret_copy(0, to, mine).wait_send()
+
+        @pl.when(jnp.logical_not(outer) & near)
+        def _():
+            aside_ret(to, across).wait_send()
+        psi_copy(1, to, mine).wait_send()
+        ret_copy(1, to, mine).wait_send()
         return c
 
     def finish_left(j, c):
@@ -252,8 +385,11 @@
     lax.fori_loop(1, half, finish, 0)
     lax.fori_loop(1, quarter, finish_left, 0)
     left_copy(left_in, across, mine, 0).wait_send()
-    for k in range(2):
-        mirror_copy(k).wait_send()
+    pieces(lambda k, q: hop_copy(k, q).wait_send())
+
+    @pl.when(jnp.logical_not(outer))
+    def _():
+        pieces(lambda k, q: mirror_copy(k, q).wait_send())
 
 
 def route(source, position, tags, psi, left, right, n, cap, lsec):
@@ -270,18 +406,20 @@
         out_specs=vmem,
         scratch_shapes=[
             pltpu.VMEM(slots, jnp.bfloat16),
-            pltpu.VMEM(slots, jnp.bfloat16),
+            pltpu.VMEM((3,) + slots[1:], jnp.bfloat16),
             pltpu.VMEM(slots, jnp.bfloat16),
             pltpu.VMEM(slots[1:], F32),
             pltpu.VMEM(right.shape, jnp.bfloat16),
             pltpu.VMEM((rsec, br, br), jnp.bfloat16),
             pltpu.VMEM((rsec, br, br), jnp.bfloat16),
+            pltpu.VMEM((rsec, br, br), jnp.bfloat16),
+            pltpu.VMEM((rsec, br, br), jnp.bfloat16),
             pltpu.VMEM((half,) + left.shape, jnp.bfloat16),
             pltpu.VMEM(tags.shape, jnp.int32),
             pltpu.SMEM(tags.shape, jnp.int32),
-            dma((2, half)), dma((2, half)), dma((2, half)), dma((2, half)),
+            dma((2, half)), dma((3, half)), dma((3, half)), dma((2, half)),
             dma((half,)), dma((half,)), dma((2, half)), dma((half,)),
-            dma((2,)), dma((2,)), dma((3,)), dma,
+            dma((2, PIECES)), dma((2, PIECES)), dma((2, PIECES)), dma((2, PIECES)), dma((3,)), dma,
         ],
         compiler_params=pltpu.CompilerParams(
             collective_id=0, has_side_effects=True, vmem_limit_bytes=56 * 1024 * 1024
@@ -313,8 +451,10 @@
     tag = (right_sector * lsec + left_sector) * (bl + 1) + block_rows
     source = jnp.sum(jnp.where(match, order[None, :], 0), axis=1)
     tags = jnp.sum(jnp.where(match, tag[None, :], 0), axis=1)
-    tags = tags.reshape(2, half, cap).transpose(1, 0, 2).reshape(half, 1, 2 * cap)
-    tags = jnp.pad(tags, ((0, 0), (0, 0), (0, -(2 * cap) % 128)))
+    tags = tags.reshape(2, half, cap)
+    tags = jnp.concatenate([tags, jnp.roll(tags[:1], half // 2, axis=1)], axis=0)
+    tags = tags.transpose(1, 0, 2).reshape(half, 1, 3 * cap)
+    tags = jnp.pad(tags, ((0, 0), (0, 0), (0, -(3 * cap) % 128)))
     left = left_env.reshape(lsec, 3 * bl, bl)
     left = jnp.concatenate([left[:, :3 * bl // 2], left[:, 3 * bl // 2:]], axis=2)
     return route(source, position, tags, psi, left, right_env, n, cap, lsec)

time: 158 us -> 154 us (0.975)
  Pallas kernels: 150 us -> 146 us
    pallas_call x1, Pallas kernels: 150 us -> 146 us  [route(): pl.pallas_call(functools.partial(route_kernel, n, lsec), out_shape=jax.Sh...]
where the time goes in v5:
time: 154 us
  Pallas kernels  146 us (95%)
  local copies, waits for them, and re-layouts  4.89 us (3%)
  other arithmetic  3.11 us (2%)
    pallas_call x1, Pallas kernels, route(): pl.pallas_call(functools.partial(route_kernel, n, lsec), out_shape=jax.Sh...  146 us
    unnamed x3, local copies, waits for them, and re-layouts  3.08 us

profile of v5, /device:TPU:0, one launch (start us, length us, event | category | flops | bytes accessed | tf_op | source)
XLA Modules:
  0.0 153.8 jit_solution(17001605537673715663)
XLA Ops:
  0.0 0.9 select_reduce_fusion.2
  0.9 0.7 multiply_add_fusion
  1.6 0.0 copy-start
  1.6 0.7 select_reduce_fusion
  2.4 0.1 slice.29
  2.5 0.1 reshape.76
  2.6 0.1 reshape.77
  2.6 0.6 pad.4.tags_in
  3.3 1.0 fusion.3
  4.2 0.7 pad_maximum_fusion.left_in
  5.0 0.0 copy-done
  5.0 145.7 %shard_map.73 = bf16[128,64,128]{2,1,0:T(8,128)(2,1)} custom-call(s32[256]{0:T(256)} %get-tuple-element.6.source, s32[128]{0:T(128)} %copy-done, s32[8,1,128]{2,1,0:T(1,128)} %pad.4.tags_in, bf16[128,64,128]{2,1,0:T(8,128)(2,1)} %psi.1, bf16[4,96,128]{2,1,0:T(8,128)(2,1)} %pad_maximum_fusion.left_in, bf16[32,2,128,128]{3,2,1,0:T(8,128)(2,1)} %right_in.1), custom_call_target="tpu_custom_call" | custom-call | flops 1879048192 | bytes 6389760 | tf_op jit(solution)/shard_map/pallas_call | solution.py:402
  150.7 3.1 %copy.14 = bf16[128,64,128]{2,1,0:T(8,128)(2,1)} copy(bf16[128,64,128]{2,1,0:T(8,128)(2,1)} %shard_map.73) | data formatting | bytes 4194304
  (4 shorter events, 0.0 us)
Async XLA Ops:
  1.6 3.3 %copy-start = (s32[128]{0:T(128)}, s32[128]{0:T(128)S(1)}, u32[]{:S(2)}) copy-start(s32[128]{0:T(128)S(1)} %get-tuple-element.12.position) | copy-start | bytes 1540
